TPU v7x, 32 devices: a whole 2x2x4 slice. The times are simulated.
32 devices in a mesh: groups: 2 (over y), gx: 8 (over z, x), gy: 2 (over core).
Axes of the slice: x: 2, y: 2, z: 4, core: 2. Of those that a mesh axis runs over, the one named last changes fastest.
Arguments:
- tokens: bfloat16 [256, 18432], P(('groups', 'gx'), 'gy'), parts along dimension 0, may hold values from -6 to 6
- up_weight: bfloat16 [40960, 18432], P('gx', 'gy'), may hold values from -0.046875 to 0.046875
Outputs:
- projected: bfloat16 [256, 40960], P(('groups', 'gy'), 'gx'), parts along dimension 0
There are 2 independent parts, one for each index of `groups`. A program takes and returns all parts, laid end to end along the dimension named above; an argument that names none is the same for every part. Nothing has to cross between parts.
All inputs are finite; a program needn't handle non-finite values.
Results may differ from a plain program's by a relative error of at most 0.001.
Values may be sent and summed in bfloat16 or wider, within the bound.
A program may use at most 192 MiB of HBM per device.

v0:
```python
import jax
import jax.numpy as jnp
from jax import lax
from jax.sharding import PartitionSpec as P


def project(rows_block, up_weight):
    return lax.dot_general(
        rows_block, up_weight, (((1,), (1,)), ((), ())), preferred_element_type=jnp.float32
    )


def on_device(tokens, up_weight):
    gathered = lax.all_gather(tokens, "gx", axis=0, tiled=True)
    partial_terms = project(gathered, up_weight)
    summed = lax.psum_scatter(partial_terms, "gy", scatter_dimension=0, tiled=True)
    return summed.astype(jnp.bfloat16)


def solution(mesh):
    placed = (P(("groups", "gx"), "gy"), P("gx", "gy"))
    return jax.shard_map(
        on_device, mesh=mesh, in_specs=placed, out_specs=P(("groups", "gy"), "gx"), check_vma=False
    )
```

profile of v0, /device:TPU:1, one launch (start us, length us, event | category | flops | bytes accessed | tf_op | source)
XLA Modules:
  0.0 122.8 jit_solution(4542534417996346340)
XLA Ops:
  6.5 0.0 all-gather.2.cloned.1.call-start
  6.5 0.7 all-gather.2.cloned.1.call-update
  7.3 0.0 reduce-scatter.2.cloned.1.call-start
  7.3 55.2 %all-gather.2.cloned.1.call-done = bf16[128,9216]{1,0:T(8,128)(2,1)} async-done(((bf16[16,9216]{1,0:T(8,128)(2,1)}), bf16[128,9216]{1,0:T(8,128)(2,1)}) %all-gather.2.cloned.1.call-update) | async-done | bytes 2359312 | tf_op jit(solution)/shard_map/all_gather | solution.py:14
  62.5 40.7 %fusion = f32[128,5120]{1,0:T(8,128)} fusion(bf16[128,9216]{1,0:T(8,128)(2,1)} %all-gather.2.cloned.1.call-done, bf16[5120,9216]{1,0:T(8,128)(2,1)} %param.3), kind=kOutput, calls=%fused_computation | convolution fusion | flops 12079595520 | bytes 99352576 | tf_op jit(solution)/shard_map/dot_general | solution.py:8
  103.2 0.0 reduce-scatter.2.cloned.1.call-update
  103.3 10.5 %reduce-scatter.2.cloned.1.call-done = f32[64,5120]{1,0:T(8,128)} async-done(((f32[128,5120]{1,0:T(8,128)}), f32[64,5120]{1,0:T(8,128)}) %reduce-scatter.2.cloned.1.call-update) | async-done | bytes 1310736 | tf_op jit(solution)/shard_map/reduce_scatter | solution.py:16
  113.8 2.2 %convert_element_type.3 = bf16[64,5120]{1,0:T(8,128)(2,1)} convert(f32[64,5120]{1,0:T(8,128)} %reduce-scatter.2.cloned.1.call-done) | non-fusion elementwise | flops 327680 | bytes 1966080 | tf_op jit(solution)/shard_map/convert_element_type | solution.py:17
Async XLA Ops:
  6.5 56.0 %all-gather.2.cloned.1.call-start = ((), (), s32[]{:S(2)}) async-start(), calls=%async_computation.1 | async-start | bytes 2654208 | tf_op jit(solution)/shard_map/all_gather | solution.py:14
  7.3 106.5 %reduce-scatter.2.cloned.1.call-start = ((), (), s32[]{:S(2)}) async-start(), calls=%async_computation.2 | async-start | bytes 3932160 | tf_op jit(solution)/shard_map/reduce_scatter | solution.py:16
Sparse Core Ops, SparseCore 0:
  9.5 52.9 all-gather.1
  103.4 10.3 reduce-scatter.1
where the time goes:
time: 123 us
  waiting for transfers between devices  66.5 us (54%)
  matrix products  40.7 us (33%)
  between operations  13.4 us (11%)
  other arithmetic  2.22 us (2%)
    all_gather x1, waiting for transfers between devices, on_device(): gathered = lax.all_gather(tokens, 'gx', axis=0, tiled=True)  55.2 us
    dot_general x1, matrix products, project(): lax.dot_general(rows_block, up_weight, (((1,), (1,)), ((), ())), preferre...  40.7 us
    reduce_scatter x1, waiting for transfers between devices, on_device(): lax.psum_scatter(partial_terms, 'gy', scatter_dimension=0, tiled=True)  10.5 us
  transfers between devices with their start and end apart: 2, of which 2 were waited for; matrix products, arithmetic and copies ran while one was open for 0% of the time, Pallas kernels for 0%

commit v1 on v0

v1 whole, which is shorter than its diff:
```python
import functools

import jax
import jax.numpy as jnp
from jax import lax
from jax.experimental import pallas as pl
from jax.experimental.pallas import tpu as pltpu
from jax.sharding import PartitionSpec as P

MESH = pl.DeviceIdType.MESH
SLACK = 0


def ring_place(index, n):
    odd, half = lax.rem(index, 2), lax.div(index, 2)
    return odd * (n - 1 - half) + (1 - odd) * half


def ring_index(place, n):
    down = lax.div(place, n // 2)
    return (1 - down) * 2 * place + down * (2 * (n - 1 - place) + 1)


def kernel(
    n, pieces, halves, tiles, slots,
    tokens_ref, weight_ref, out_ref,
    gathered, weights, acc, parts, arrived, result,
    own_sem, weight_sem, send_sem, recv_sem, part_send, part_recv, out_sem,
):
    me, core = lax.axis_index("gx"), lax.axis_index("gy")
    rows, width = tokens_ref.shape[0], gathered.shape[2]
    block, tile = weights.shape[1], weights.shape[1] // tiles
    hops = n // 2
    place = ring_place(me, n)
    neighbours = tuple(ring_index(lax.rem(place + d, n), n) for d in (1, n - 1))
    blocks = pieces * halves

    def weight_copy(piece, half):
        slot = lax.rem(piece * halves + half, slots)
        return pltpu.make_async_copy(
            weight_ref.at[
                pl.ds(half * block, block), pl.ds(pl.multiple_of(piece * width, 128), width)
            ],
            weights.at[slot],
            weight_sem.at[slot],
        )

    def own_columns(piece):
        return tokens_ref.at[:, pl.ds(pl.multiple_of(piece * width, 128), width)]

    def rows_of(owner):
        return pl.ds(pl.multiple_of(owner * rows, rows), rows)

    def own_copy(piece):
        return pltpu.make_async_copy(
            own_columns(piece), gathered.at[piece, rows_of(me)], own_sem.at[piece]
        )

    def ring_copy(way, piece, hop):
        back = n - hop if way == 0 else hop
        held = gathered.at[piece, rows_of(ring_index(lax.rem(place + back, n), n))]
        return pltpu.make_async_remote_copy(
            src_ref=own_columns(piece) if hop == 0 else held,
            dst_ref=held,
            send_sem=send_sem.at[way, piece, hop],
            recv_sem=recv_sem.at[way, piece, hop],
            device_id={"gx": neighbours[way]},
            device_id_type=MESH,
        )

    def each_way(piece, hop, act):
        if hop < hops - 1:
            act(0)
            act(1)
        elif isinstance(piece, int):
            act(piece % 2)
        else:
            pl.when(lax.rem(piece, 2) == 0)(lambda: act(0))
            pl.when(lax.rem(piece, 2) == 1)(lambda: act(1))

    def stage(piece, hop):
        if hop >= 1:
            each_way(piece, hop - 1, lambda way: ring_copy(way, piece, hop - 1).wait_recv())
        if hop < hops:
            each_way(piece, hop, lambda way: ring_copy(way, piece, hop).start())

    def tick(step, extra):
        for hop in range(hops, -1, -1):
            if (extra - hop) % halves:
                continue
            piece = step + (extra - hop) // halves
            if isinstance(step, int):
                if 0 <= piece < pieces:
                    stage(piece, hop)
            else:
                pl.when(piece < pieces)(functools.partial(stage, piece, hop))

    for b in range(min(slots, blocks)):
        weight_copy(b // halves, b % halves).start()

    barrier = pltpu.get_barrier_semaphore()
    for neighbour in neighbours:
        pl.semaphore_signal(barrier, inc=1, device_id={"gx": neighbour}, device_id_type=MESH)
    pl.semaphore_signal(barrier, inc=1, device_id={"gy": 1 - core}, device_id_type=MESH)
    pl.semaphore_wait(barrier, 3)

    ahead = hops + SLACK
    tick(0, 0)
    for piece in range(pieces):
        own_copy(piece).start()
    for t in range(1, ahead):
        tick(t // halves, t % halves)
    acc[...] = jnp.zeros_like(acc)

    def product(piece, half, tile_at):
        slot = lax.rem(piece * halves + half, slots)
        at = pl.ds(tile_at[0], tile_at[1])
        return lax.dot_general(
            weights[slot, at, :], gathered[piece], (((1,), (1,)), ((), ())),
            preferred_element_type=jnp.float32,
        )

    @pl.loop(0, pieces - 1)
    def _(piece):
        for half in range(halves):
            tick(piece, half + ahead)
            if half == 0:
                own_copy(piece).wait()
            weight_copy(piece, half).wait()
            acc[pl.ds(half * block, block), :] += product(piece, half, (0, block))
            later = piece * halves + half + slots

            @pl.when(later < blocks)
            def _():
                weight_copy(lax.div(later, halves), lax.rem(later, halves)).start()

    last = pieces - 1
    for extra in range(halves):
        tick(last, extra + ahead)
    own_copy(last).wait()
    mine = parts.shape[1]

    def part_copy(j):
        at = pl.ds(j * tile, tile)
        return pltpu.make_async_remote_copy(
            src_ref=parts.at[1 - core, :, at],
            dst_ref=arrived.at[:, at],
            send_sem=part_send.at[j],
            recv_sem=part_recv.at[j],
            device_id={"gy": 1 - core},
            device_id_type=MESH,
        )

    def out_copy(j):
        at = pl.ds(j * tile, tile)
        return pltpu.make_async_copy(result.at[:, at], out_ref.at[:, at], out_sem.at[j])

    def combine(j):
        at = pl.ds(j * tile, tile)
        part_copy(j).wait_recv()
        result[:, at] = (parts[core, :, at] + arrived[:, at]).astype(result.dtype)
        out_copy(j).start()

    total = halves * tiles
    for j in range(total):
        half, within = j // tiles, j % tiles
        if within == 0:
            weight_copy(last, half).wait()
        summed = acc[pl.ds(j * tile, tile), :] + product(last, half, (within * tile, tile))
        turned = summed.T
        at = pl.ds(j * tile, tile)
        parts[0, :, at] = turned[:mine]
        parts[1, :, at] = turned[mine:]
        part_copy(j).start()
        if j >= 2:
            combine(j - 2)
    for j in range(max(total - 2, 0), total):
        combine(j)

    @pl.loop(0, pieces)
    def _(piece):
        for hop in range(hops):
            each_way(piece, hop, lambda way: ring_copy(way, piece, hop).wait_send())

    for j in range(total):
        part_copy(j).wait_send()
        out_copy(j).wait()


def on_device(n, tokens, up_weight):
    rows, depth = tokens.shape
    hidden = up_weight.shape[0]
    width = 1024 if depth % 1024 == 0 else 128
    pieces = depth // width
    halves = 2 if hidden % 256 == 0 else 1
    block = hidden // halves
    tiles = 2 if block % 256 == 0 else 1
    slots = min(8, pieces * halves)
    every, mine = rows * n, rows * n // 2
    dma = pltpu.SemaphoreType.DMA
    return pl.pallas_call(
        functools.partial(kernel, n, pieces, halves, tiles, slots),
        out_shape=jax.ShapeDtypeStruct((mine, hidden), jnp.bfloat16),
        in_specs=[pl.BlockSpec(memory_space=pl.ANY)] * 2,
        out_specs=pl.BlockSpec(memory_space=pl.ANY),
        scratch_shapes=[
            pltpu.VMEM((pieces, every, width), jnp.bfloat16),
            pltpu.VMEM((slots, block, width), jnp.bfloat16),
            pltpu.VMEM((hidden, every), jnp.float32),
            pltpu.VMEM((2, mine, hidden), jnp.float32),
            pltpu.VMEM((mine, hidden), jnp.float32),
            pltpu.VMEM((mine, hidden), jnp.bfloat16),
            dma((pieces,)),
            dma((slots,)),
            dma((2, pieces, n // 2)),
            dma((2, pieces, n // 2)),
            dma((halves * tiles,)),
            dma((halves * tiles,)),
            dma((halves * tiles,)),
        ],
        compiler_params=pltpu.CompilerParams(
            collective_id=0, has_side_effects=True, vmem_limit_bytes=58 * 2**20
        ),
        cost_estimate=pl.CostEstimate(
            flops=2 * every * hidden * depth, bytes_accessed=2 * hidden * depth, transcendentals=0
        ),
    )(tokens, up_weight)


def solution(mesh):
    placed = (P(("groups", "gx"), "gy"), P("gx", "gy"))
    return jax.shard_map(
        functools.partial(on_device, mesh.shape["gx"]),
        mesh=mesh,
        in_specs=placed,
        out_specs=P(("groups", "gy"), "gx"),
        check_vma=False,
    )
```

time: 123 us -> 77.8 us (0.63)
  Pallas kernels: 0 us -> 75.7 us
  waiting for transfers between devices: 66.5 us -> 0 us
  matrix products: 40.7 us -> 0 us
  between operations: 13.4 us -> 0.01 us
  other arithmetic: 2.22 us -> 0 us
  local copies, waits for them, and re-layouts: 0 us -> 1.97 us
    pallas_call x0 -> x1, Pallas kernels: none -> 75.7 us  [on_device(): pl.pallas_call(functools.partial(kernel, n, pieces, halves, tiles, slots)...]
    all_gather x1 -> x0, waiting for transfers between devices: 55.2 us -> none  [on_device(): gathered = lax.all_gather(tokens, 'gx', axis=0, tiled=True)]
    dot_general x1 -> x0, matrix products: 40.7 us -> none  [project(): lax.dot_general(rows_block, up_weight, (((1,), (1,)), ((), ())), preferre...]
    reduce_scatter x1 -> x0, waiting for transfers between devices: 10.5 us -> none  [on_device(): lax.psum_scatter(partial_terms, 'gy', scatter_dimension=0, tiled=True)]
    convert_element_type x1 -> x0, other arithmetic: 2.22 us -> none  [on_device(): return summed.astype(jnp.bfloat16)]
    unnamed x0 -> x1, local copies, waits for them, and re-layouts: none -> 1.97 us
  transfers between devices with their start and end apart: 2 -> 0, of which waited for: 2 -> 0; matrix products, arithmetic and copies ran while one was open for 0% -> 0% of each run, Pallas kernels for 0% -> 0%
where the time goes in v1:
time: 77.8 us; the launch traced here: 77.7 us
  Pallas kernels  75.7 us (97%)
  local copies, waits for them, and re-layouts  1.97 us (3%)
    pallas_call x1, Pallas kernels, on_device(): pl.pallas_call(functools.partial(kernel, n, pieces, halves, tiles, slots)...  75.7 us
    unnamed x1, local copies, waits for them, and re-layouts  1.97 us

profile of v1, /device:TPU:1, one launch (start us, length us, event | category | flops | bytes accessed | tf_op | source)
XLA Modules:
  0.0 77.7 jit_solution(4223136243852124524)
XLA Ops:
  0.0 75.7 %shard_map.28 = bf16[64,5120]{1,0:T(8,128)(2,1)} custom-call(bf16[16,9216]{1,0:T(8,128)(2,1)} %tokens_ref.1, bf16[5120,9216]{1,0:T(8,128)(2,1)} %weight_ref.1), custom_call_target="tpu_custom_call" | custom-call | flops 12079595520 | bytes 94371840 | tf_op jit(solution)/shard_map/pallas_call | solution.py:201
  75.7 2.0 %copy.4 = bf16[64,5120]{1,0:T(8,128)(2,1)} copy(bf16[64,5120]{1,0:T(8,128)(2,1)} %shard_map.28) | data formatting | bytes 1310720

commit v2 on v1

--- a/solution.py
+++ b/solution.py
@@ -9,6 +9,7 @@
 
 MESH = pl.DeviceIdType.MESH
 SLACK = 0
+LAG = 3
 
 
 def ring_place(index, n):
@@ -86,9 +87,9 @@
 
     def tick(step, extra):
         for hop in range(hops, -1, -1):
-            if (extra - hop) % halves:
+            if (extra - hop * LAG) % halves:
                 continue
-            piece = step + (extra - hop) // halves
+            piece = step + (extra - hop * LAG) // halves
             if isinstance(step, int):
                 if 0 <= piece < pieces:
                     stage(piece, hop)
@@ -104,7 +105,7 @@
     pl.semaphore_signal(barrier, inc=1, device_id={"gy": 1 - core}, device_id_type=MESH)
     pl.semaphore_wait(barrier, 3)
 
-    ahead = hops + SLACK
+    ahead = hops * LAG + SLACK
     tick(0, 0)
     for piece in range(pieces):
         own_copy(piece).start()

time: 77.8 us -> 52.4 us (0.67)
  Pallas kernels: 75.7 us -> 50.2 us
    pallas_call x1, Pallas kernels: 75.7 us -> 50.2 us  [on_device(): pl.pallas_call(functools.partial(kernel, n, pieces, halves, tiles, slots)...]
where the time goes in v2:
time: 52.4 us; the launch traced here: 52.2 us
  Pallas kernels  50.2 us (96%)
  local copies, waits for them, and re-layouts  1.97 us (4%)
    pallas_call x1, Pallas kernels, on_device(): pl.pallas_call(functools.partial(kernel, n, pieces, halves, tiles, slots)...  50.2 us
    unnamed x1, local copies, waits for them, and re-layouts  1.97 us

profile of v2, /device:TPU:1, one launch (start us, length us, event | category | flops | bytes accessed | tf_op | source)
XLA Modules:
  0.0 52.2 jit_solution(14398122024960968523)
XLA Ops:
  0.0 50.2 %shard_map.28 = bf16[64,5120]{1,0:T(8,128)(2,1)} custom-call(bf16[16,9216]{1,0:T(8,128)(2,1)} %tokens_ref.1, bf16[5120,9216]{1,0:T(8,128)(2,1)} %weight_ref.1), custom_call_target="tpu_custom_call" | custom-call | flops 12079595520 | bytes 94371840 | tf_op jit(solution)/shard_map/pallas_call | solution.py:202
  50.3 2.0 %copy.4 = bf16[64,5120]{1,0:T(8,128)(2,1)} copy(bf16[64,5120]{1,0:T(8,128)(2,1)} %shard_map.28) | data formatting | bytes 1310720
